TPU v7x, 512 devices: a whole 4x8x8 slice. The times are simulated.
512 devices in a mesh: dp: 64 (over z, y_lo, x), tensor: 8 (over y_hi, core).
Axes of the slice: x: 4, y: 8 (y_hi: 4, y_lo: 2; y = y_hi * 2 + y_lo), z: 8, core: 2. Of those that a mesh axis runs over, the one named last changes fastest.
Arguments:
- current_acts: bfloat16 [49152, 4096], P('dp', 'tensor'), may hold values from -70 to 70
- current_cot: bfloat16 [49152, 1024], P('dp', 'tensor'), may hold values from -56 to 56
- current_ids: int32 [49152], P('dp'), may hold values from 0 to 128004, as said below
- replay_acts: bfloat16 [49152, 4096], P('dp', 'tensor'), may hold values from -92 to 92
- replay_cot: bfloat16 [49152, 1024], P('dp', 'tensor'), may hold values from -70 to 70
- replay_ids: int32 [49152], P('dp'), may hold values from 0 to 128004, as said below
- master_weight: float32 [4096, 1024], P('dp', 'tensor'), may hold values from -0.09375 to 0.09375
- first_moment: float32 [4096, 1024], P('dp', 'tensor'), may hold values from -0.75 to 0.75
- second_moment: float32 [4096, 1024], P('dp', 'tensor'), may hold values from 1e-05 to 0.1
Outputs:
- new_master: float32 [4096, 1024], P('dp', 'tensor')
- new_first: float32 [4096, 1024], P('dp', 'tensor')
- new_second: float32 [4096, 1024], P('dp', 'tensor')
- gathered_weight: bfloat16 [4096, 1024], P(None, 'tensor')
Inputs may be any that keep to these rules, and one draw needn't show every extreme that they name: `current_ids`: the first token of every 768 consecutive tokens is never 128004; other ids are below 128004. `replay_ids`: the first token of every 768 consecutive tokens is never 128004; other ids are below 128004.
All inputs are finite; a program needn't handle non-finite values.
Results may differ from a plain program's by a relative error of at most 0.001.
Values may be sent and summed in bfloat16 or wider, within the bound.
A program may use at most 64 MiB of HBM per device.

v0:
```python
import jax
import jax.numpy as jnp
from jax import lax
from jax.sharding import PartitionSpec as P

PAD_ID = 128004


beta_first = 0.9
beta_second = 0.95
adam_eps = 1e-08
learn_rate = 0.001
decay_rate = 0.1
step_number = 10.0
norm_eps = 1e-12


def contract(activations, cotangent):
    return lax.dot_general(
        activations, cotangent, (((0,), (0,)), ((), ())), preferred_element_type=jnp.float32
    )


def gather_heads(current_cot, replay_cot):
    return (
        lax.all_gather(current_cot, "tensor", axis=1, tiled=True),
        lax.all_gather(replay_cot, "tensor", axis=1, tiled=True),
    )


def reduce_rows(first_part, second_part):
    return (
        lax.psum_scatter(first_part, "dp", scatter_dimension=0, tiled=True),
        lax.psum_scatter(second_part, "dp", scatter_dimension=0, tiled=True),
    )


def on_device(
    current_acts,
    current_cot,
    current_ids,
    replay_acts,
    replay_cot,
    replay_ids,
    master_weight,
    first_moment,
    second_moment,
):
    kept_current = (current_ids != PAD_ID).astype(jnp.bfloat16)
    kept_replay = (replay_ids != PAD_ID).astype(jnp.bfloat16)
    cot_current, cot_replay = gather_heads(current_cot, replay_cot)
    part_current = contract(current_acts, cot_current * kept_current[:, None])
    part_replay = contract(replay_acts, cot_replay * kept_replay[:, None])
    part_current, part_replay = (
        lax.all_to_all(part_current, "tensor", split_axis=1, concat_axis=0, tiled=True),
        lax.all_to_all(part_replay, "tensor", split_axis=1, concat_axis=0, tiled=True),
    )
    summed_current, replay_grad = reduce_rows(part_current, part_replay)
    local_count = jnp.sum(kept_current.astype(jnp.float32))
    valid_count = lax.psum(local_count, "dp")
    current_grad = summed_current / valid_count
    inner_sum, energy = lax.psum(
        (jnp.sum(current_grad * replay_grad), jnp.sum(replay_grad * replay_grad)), ("dp", "tensor")
    )
    projected = current_grad - jnp.minimum(inner_sum, 0.0) / (energy + norm_eps) * replay_grad
    new_first = beta_first * first_moment + (1.0 - beta_first) * projected
    new_second = beta_second * second_moment + (1.0 - beta_second) * projected * projected
    fix_first = 1.0 - beta_first**step_number
    fix_second = 1.0 - beta_second**step_number
    update = new_first / fix_first / (jnp.sqrt(new_second / fix_second) + adam_eps)
    new_master = master_weight - learn_rate * (update + decay_rate * master_weight)
    gathered_weight = lax.all_gather(new_master.astype(jnp.bfloat16), "dp", axis=0, tiled=True)
    return (new_master, new_first, new_second, gathered_weight)


def solution(mesh):
    placed = (
        P("dp", "tensor"),
        P("dp", "tensor"),
        P("dp"),
        P("dp", "tensor"),
        P("dp", "tensor"),
        P("dp"),
        P("dp", "tensor"),
        P("dp", "tensor"),
        P("dp", "tensor"),
    )
    return jax.shard_map(
        on_device,
        mesh=mesh,
        in_specs=placed,
        out_specs=(P("dp", "tensor"), P("dp", "tensor"), P("dp", "tensor"), P(None, "tensor")),
        check_vma=False,
    )
```

profile of v0, /device:TPU:16, one launch (start us, length us, event | category | flops | bytes accessed | tf_op | source)
XLA Modules:
  0.0 1186.7 jit_solution(7463575644486137855)
XLA Ops:
  7.2 0.0 copy-start
  7.2 0.0 all-gather.4.cloned.1.call-start
  7.2 0.7 all-gather.4.cloned.1.call-update
  7.9 1.3 convert_reduce_fusion
  9.2 43.7 %all-gather.4.cloned.1.call-done = bf16[768,1024]{1,0:T(8,128)(2,1)} async-done(((bf16[768,128]{1,0:T(8,128)(2,1)}), bf16[768,1024]{1,0:T(8,128)(2,1)}) %all-gather.4.cloned.1.call-update) | async-done | bytes 1572880 | tf_op jit(solution)/shard_map/all_gather | solution.py:26
  52.9 0.0 copy-done
  52.9 3.9 fusion.2
  56.8 4.9 all-to-all-start
  61.7 0.0 all-gather.6.cloned.1.call-start
  61.7 0.7 all-gather.6.cloned.1.call-update
  62.4 0.0 reduce-scatter.3.cloned.1.call-start
  62.5 59.9 %all-to-all-done = f32[512,8,128]{0,2,1:T(8,128)S(1)} async-done(((f32[512,8,128]{0,2,1:T(8,128)}), f32[512,8,128]{0,2,1:T(8,128)S(1)}, u32[]{:S(2)}, u32[]{:S(2)}) %all-to-all-start) | async-done | bytes 2097184 | tf_op jit(solution)/shard_map/all_to_all | solution.py:55
  122.4 1.9 copy.13
  124.2 0.0 copy-start.4
  124.2 0.0 copy-start.5
  124.2 0.0 reduce-scatter.3.cloned.1.call-update
  124.3 0.0 reduce-scatter.5.cloned.1.call-start
  124.3 0.6 copy-done.4
  124.9 0.0 all-gather.6.cloned.1.call-done
  124.9 0.5 copy-done.5
  125.4 2.5 fusion
  127.9 56.8 %all_to_all.38 = f32[512,8,128]{0,2,1:T(8,128)S(1)} all-to-all(f32[512,8,128]{0,2,1:T(8,128)S(1)} %bitcast.17), channel_id=1, replica_groups=mesh['dp'=64,'tensor'=8] {'tensor'}, dimensions={1} | all-to-all | bytes 4194304 | tf_op jit(solution)/shard_map/all_to_all | solution.py:56
  184.7 1.8 copy.14
  186.6 0.0 copy-start.1
  186.6 0.0 copy-start.2
  186.6 0.0 copy-start.3
  186.6 0.0 reduce-scatter.5.cloned.1.call-update
  186.6 0.0 all-gather.8.cloned.1.call-start
  186.6 154.3 %psum.21 = f32[]{:T(128)} all-reduce(f32[]{:T(128)} %get-tuple-element.12), channel_id=1, replica_groups=mesh['dp'=64,'tensor'=8] {'dp'}, use_global_device_ids=true, to_apply=%region_2.0 | all-reduce | flops 1 | bytes 8 | tf_op jit(solution)/shard_map/psum | solution.py:60
  341.0 118.5 %reduce-scatter.3.cloned.1.call-done = f32[64,128]{1,0:T(8,128)} async-done(((f32[4096,128]{1,0:T(8,128)}), f32[64,128]{1,0:T(8,128)}) %reduce-scatter.3.cloned.1.call-update) | async-done | bytes 32784 | tf_op jit(solution)/shard_map/reduce_scatter | solution.py:33
  459.5 323.3 %reduce-scatter.5.cloned.1.call-done = f32[64,128]{1,0:T(8,128)} async-done(((f32[4096,128]{1,0:T(8,128)}), f32[64,128]{1,0:T(8,128)}) %reduce-scatter.5.cloned.1.call-update) | async-done | bytes 32784 | tf_op jit(solution)/shard_map/reduce_scatter | solution.py:34
  782.7 2.1 multiply_reduce_fusion
  784.8 92.5 %all-reduce = (f32[]{:T(128)}, f32[]{:T(128)}) all-reduce(f32[]{:T(128)} %get-tuple-element.5, f32[]{:T(128)} %get-tuple-element.4), channel_id=1, replica_groups=mesh['dp'=64,'tensor'=8] {'dp','tensor'}, use_global_device_ids=true, to_apply=%region_5.0 | all-reduce | flops 2 | bytes 16 | tf_op jit(solution)/shard_map/psum | solution.py:62
  878.6 0.0 copy-done.1
  878.7 0.0 copy-done.2
  878.7 0.0 copy-done.3
  878.7 2.1 fusion.7
  880.8 0.0 all-gather.8.cloned.1.call-update
  880.8 297.1 %all-gather.8.cloned.1.call-done = bf16[4096,128]{1,0:T(8,128)(2,1)} async-done(((bf16[64,128]{1,0:T(8,128)(2,1)}), bf16[4096,128]{1,0:T(8,128)(2,1)}) %all-gather.8.cloned.1.call-update) | async-done | bytes 1048592 | tf_op jit(solution)/shard_map/all_gather | solution.py:72
  1177.9 2.3 copy.16
  (1 shorter events, 0.0 us)
Async XLA Ops:
  7.2 45.8 %copy-start = (bf16[768,512]{1,0:T(8,128)(2,1)S(1)}, bf16[768,512]{1,0:T(8,128)(2,1)}, u32[]{:S(2)}) copy-start(bf16[768,512]{1,0:T(8,128)(2,1)} %param.9) | copy-start | bytes 2359300
  7.2 45.8 %all-gather.4.cloned.1.call-start = ((), (), s32[]{:S(2)}) async-start(), calls=%async_computation.4 | async-start | bytes 1769472 | tf_op jit(solution)/shard_map/all_gather | solution.py:26
  56.8 65.6 %all-to-all-start = ((f32[512,8,128]{0,2,1:T(8,128)}), f32[512,8,128]{0,2,1:T(8,128)S(1)}, u32[]{:S(2)}, u32[]{:S(2)}) async-start(f32[512,8,128]{0,2,1:T(8,128)} %bitcast.16), calls=%async_computation | async-start | bytes 4194304 | tf_op jit(solution)/shard_map/all_to_all | solution.py:55
  61.7 63.2 %all-gather.6.cloned.1.call-start = ((), (), s32[]{:S(2)}) async-start(), calls=%async_computation.6 | async-start | bytes 1769472 | tf_op jit(solution)/shard_map/all_gather | solution.py:27
  62.4 397.0 %reduce-scatter.3.cloned.1.call-start = ((), (), s32[]{:S(2)}) async-start(), calls=%async_computation.5 | async-start | bytes 2129920 | tf_op jit(solution)/shard_map/reduce_scatter | solution.py:33
  124.2 0.7 copy-start.4
  124.2 1.1 copy-start.5
  124.3 658.5 %reduce-scatter.5.cloned.1.call-start = ((), (), s32[]{:S(2)}) async-start(), calls=%async_computation.7 | async-start | bytes 2129920 | tf_op jit(solution)/shard_map/reduce_scatter | solution.py:34
  186.6 692.1 %copy-start.1 = (f32[64,128]{1,0:T(8,128)S(1)}, f32[64,128]{1,0:T(8,128)}, u32[]{:S(2)}) copy-start(f32[64,128]{1,0:T(8,128)} %param.15) | copy-start | bytes 98308
  186.6 692.1 %copy-start.2 = (f32[64,128]{1,0:T(8,128)S(1)}, f32[64,128]{1,0:T(8,128)}, u32[]{:S(2)}) copy-start(f32[64,128]{1,0:T(8,128)} %param.16) | copy-start | bytes 98308
  186.6 692.1 %copy-start.3 = (f32[64,128]{1,0:T(8,128)S(1)}, f32[64,128]{1,0:T(8,128)}, u32[]{:S(2)}) copy-start(f32[64,128]{1,0:T(8,128)} %param.17) | copy-start | bytes 98308
  186.6 991.3 %all-gather.8.cloned.1.call-start = ((), (), s32[]{:S(2)}) async-start(), calls=%async_computation.8 | async-start | bytes 1064960 | tf_op jit(solution)/shard_map/all_gather | solution.py:72
Sparse Core Ops, SparseCore 0:
  10.1 42.7 all-gather.3
  64.6 59.1 all-gather.5
  126.7 332.7 reduce-scatter.2
  462.3 320.3 reduce-scatter.4
  880.9 296.9 all-gather.7
where the time goes:
time: 1190 us
  waiting for transfers between devices  844 us (71%)
  blocking collectives  304 us (26%)
  between operations  15.2 us (1%)
    reduce_scatter x1, waiting for transfers between devices, reduce_rows(): lax.psum_scatter(second_part, 'dp', scatter_dimension=0, tiled=True)  323 us
    all_gather x1, waiting for transfers between devices, on_device(): lax.all_gather(new_master.astype(jnp.bfloat16), 'dp', axis=0, tiled=True)  297 us
    psum x1, blocking collectives, on_device(): valid_count = lax.psum(local_count, 'dp')  154 us
    reduce_scatter x1, waiting for transfers between devices, reduce_rows(): lax.psum_scatter(first_part, 'dp', scatter_dimension=0, tiled=True)  118 us
    psum x1, blocking collectives, on_device(): lax.psum((jnp.sum(current_grad * replay_grad), jnp.sum(replay_grad * repl...  92.5 us
    all_to_all x1, waiting for transfers between devices, on_device(): lax.all_to_all(part_current, 'tensor', split_axis=1, concat_axis=0, tiled...  59.9 us
    all_to_all x1, blocking collectives, on_device(): lax.all_to_all(part_replay, 'tensor', split_axis=1, concat_axis=0, tiled=...  56.8 us
    all_gather x1, waiting for transfers between devices, gather_heads(): lax.all_gather(current_cot, 'tensor', axis=1, tiled=True)  43.7 us
  transfers between devices with their start and end apart: 6, of which 5 were waited for; matrix products, arithmetic and copies ran while one was open for 1% of the time, Pallas kernels for 0%

commit v1 on v0

v1 whole, which is shorter than its diff:
```python
import jax
import jax.numpy as jnp
from jax import lax
from jax.experimental import pallas as pl
from jax.experimental.pallas import tpu as pltpu
from jax.sharding import PartitionSpec as P

PAD_ID = 128004
TOK = 768
FEAT = 512
HEAD = 128
ROWS = 64

beta_first = 0.9
beta_second = 0.95
adam_eps = 1e-08
learn_rate = 0.001
decay_rate = 0.1
step_number = 10.0
norm_eps = 1e-12

MESH = pl.DeviceIdType.MESH
HALF = TOK // 2

OWN, LOW, HIGH, FAR = range(4)
SHIFT = (0, 3, 1, 2)
ORDER = (
    (0, OWN),
    (1, OWN),
    (0, LOW),
    (0, HIGH),
    (0, FAR),
    (1, LOW),
    (1, HIGH),
    (1, FAR),
)


def kernel(
    cur_acts,
    cur_cot,
    cur_ids,
    rep_acts,
    rep_cot,
    rep_ids,
    master,
    first,
    second,
    new_master,
    new_first,
    new_second,
    gathered,
    acts,
    acts_t,
    cots,
    part_own,
    part_out,
    x_in,
    z_out,
    z_in,
    f_out,
    f_in,
    state,
    scal,
    load_sem,
    pair_send,
    pair_recv,
    y_send,
    y_recv,
    x_send,
    x_recv,
    z_send,
    z_recv,
    f_send,
    f_recv,
    s_send,
    s_recv,
    g_send,
    g_recv,
):
    dp = lax.axis_index("dp")
    tensor = lax.axis_index("tensor")
    z, yl, x = dp // 8, (dp // 4) % 2, dp % 4
    yh, c = tensor // 2, tensor % 2

    def device(z=z, yl=yl, x=x, yh=yh, c=c):
        return (z * 8 + yl * 4 + x, yh * 2 + c)

    def remote(src, dst, send, recv, target):
        return pltpu.make_async_remote_copy(
            src_ref=src,
            dst_ref=dst,
            send_sem=send,
            recv_sem=recv,
            device_id=target,
            device_id_type=MESH,
        )

    def z_peer(d):
        return device(z=(z + d) % 8)

    def x_peer(d):
        return device(x=(x + d) % 4)

    def xc_peer(d):
        return device(x=(x + d // 2) % 4, c=(c + d % 2) % 2)

    def y_peer(d):
        return device(yh=(yh + d // 2) % 4, yl=(yl + d % 2) % 2)

    act_refs, cot_refs, id_refs = (
        (cur_acts, rep_acts),
        (cur_cot, rep_cot),
        (cur_ids, rep_ids),
    )
    act_loads = [
        pltpu.make_async_copy(act_refs[b], acts.at[b], load_sem.at[b]) for b in range(2)
    ]
    cot_loads = [
        pltpu.make_async_copy(cot_refs[b], cots.at[b, OWN], load_sem.at[2 + b])
        for b in range(2)
    ]
    state_loads = [
        pltpu.make_async_copy(ref, state.at[i], load_sem.at[4 + i])
        for i, ref in enumerate((master, first, second))
    ]
    for copy in act_loads + cot_loads + state_loads:
        copy.start()

    goal_z, goal_yl = 2 * yh + z // 4, (z // 2) % 2
    goal_self = (goal_z == z) & (goal_yl == yl)

    barrier = pltpu.get_barrier_semaphore()
    for d in range(1, 8):
        for peer in (z_peer(d), xc_peer(d), y_peer(d)):
            pl.semaphore_signal(barrier, inc=1, device_id=peer, device_id_type=MESH)
    for q in range(2):
        for other in range(2):
            origin_z, origin_yh = (z % 2) * 4 + yl * 2 + q, z // 2
            origin_self = (origin_z == z) & (origin_yh == yh) & (yl == other)

            @pl.when(jnp.logical_not(origin_self))
            def _():
                pl.semaphore_signal(
                    barrier,
                    inc=1,
                    device_id=device(z=origin_z, yl=other, yh=origin_yh),
                    device_id_type=MESH,
                )

    @pl.when(goal_self)
    def _():
        pl.semaphore_wait(barrier, 24)

    @pl.when(jnp.logical_not(goal_self))
    def _():
        pl.semaphore_wait(barrier, 25)

    def half(h):
        return pl.ds(h * HALF, HALF)

    right, left = device(yh=(yh + 1) % 4), device(yh=(yh + 3) % 4)

    def to_right(b, h):
        return remote(
            cot_refs[b].at[half(h)],
            cots.at[b, LOW, half(h)],
            y_send.at[b, 0, h],
            y_recv.at[b, 0, h],
            right,
        )

    def to_left(b, h):
        return remote(
            cot_refs[b].at[half(h)],
            cots.at[b, HIGH, half(h)],
            y_send.at[b, 1, h],
            y_recv.at[b, 1, h],
            left,
        )

    def on_right(b):
        return remote(
            cots.at[b, LOW, half(0)],
            cots.at[b, FAR, half(0)],
            y_send.at[b, 2, 0],
            y_recv.at[b, 2, 0],
            right,
        )

    def on_left(b):
        return remote(
            cots.at[b, HIGH, half(1)],
            cots.at[b, FAR, half(1)],
            y_send.at[b, 2, 1],
            y_recv.at[b, 2, 1],
            left,
        )

    def send_own(b):
        to_right(b, 0).start()
        to_left(b, 1).start()
        to_right(b, 1).start()
        to_left(b, 0).start()

    def forward(b):
        to_right(b, 0).wait_recv()
        on_right(b).start()
        to_left(b, 1).wait_recv()
        on_left(b).start()

    send_own(0)

    def pair(b):
        return remote(
            acts_t.at[b, c],
            acts_t.at[b, c],
            pair_send.at[b],
            pair_recv.at[b],
            device(c=1 - c),
        )

    def pair_in(b):
        return remote(
            acts_t.at[b, 1 - c],
            acts_t.at[b, 1 - c],
            pair_send.at[b],
            pair_recv.at[b],
            device(c=1 - c),
        )

    def kept(b):
        return (id_refs[b][...] != PAD_ID).astype(jnp.float32)

    for b in range(2):
        act_loads[b].wait()
        mask = kept(b).astype(jnp.bfloat16)
        for j in range(4):
            block = acts[b, :, pl.ds(j * 128, 128)].T * mask
            for part in range(2):
                acts_t[b, c, 2 * (j % 2) + part, pl.ds((j // 2) * ROWS, ROWS), :] = (
                    block[part * ROWS : (part + 1) * ROWS]
                )
        pair(b).start()

    def x_copy(b, rel, d):
        return remote(
            part_out.at[b, rel, d],
            x_in.at[b, rel, d],
            x_send.at[b, rel, d],
            x_recv.at[b, rel, d],
            x_peer(d),
        )

    def multiply(b, rel):
        cot = cots[b, rel]
        for d in (2, 1, 3, 0):
            block = (x + d) % 4
            for group in range(2):
                tile = jnp.dot(
                    acts_t[b, group, block], cot, preferred_element_type=jnp.float32
                )
                rows = pl.ds(group * 128, 128)
                if d:
                    part_out[b, rel, d, rows] = tile.astype(jnp.bfloat16)
                else:
                    part_own[b, rel, rows] = tile
            if d:
                x_copy(b, rel, d).start()

    def z_copy(b, rel, d):
        return remote(
            z_out.at[b, rel, (z + d) % 8],
            z_in.at[b, rel, d],
            z_send.at[b, rel, d],
            z_recv.at[b, rel, d],
            z_peer(d),
        )

    def add_x(b, rel):
        for d in range(1, 4):
            x_copy(b, rel, d).wait_recv()
        total = part_own[b, rel]
        for d in range(1, 4):
            total = total + x_in[b, rel, d].astype(jnp.float32)
        z_out[b, rel] = total.reshape(8, 32, 128)
        for d in (4, 3, 5, 2, 6, 1, 7):
            z_copy(b, rel, d).start()

    def goal(rel):
        return device(z=goal_z, yl=goal_yl, yh=(yh + SHIFT[rel]) % 4)

    def f_copy(b, rel):
        return remote(
            f_out.at[b, rel],
            f_in.at[b, yl, z % 2],
            f_send.at[b, rel],
            f_recv.at[b, yl, z % 2],
            goal(rel),
        )

    def f_local(b):
        return pltpu.make_async_copy(
            f_out.at[b, OWN], f_in.at[b, yl, z % 2], f_recv.at[b, yl, z % 2]
        )

    def add_z(b, rel):
        for d in range(1, 8):
            z_copy(b, rel, d).wait_recv()
        total = z_out[b, rel, z]
        for d in range(1, 8):
            total = total + z_in[b, rel, d]
        f_out[b, rel] = total
        if rel == OWN:

            @pl.when(goal_self)
            def _():
                f_local(b).start()

            @pl.when(jnp.logical_not(goal_self))
            def _():
                f_copy(b, rel).start()

        else:
            f_copy(b, rel).start()

    def arrive(b, rel):
        if rel == OWN:
            cot_loads[b].wait()
            pair_in(b).wait_recv()
        elif rel == LOW:
            if b == 0:
                forward(0)
                send_own(1)
            else:
                forward(1)
            to_right(b, 1).wait_recv()
        elif rel == HIGH:
            to_left(b, 0).wait_recv()
        else:
            on_right(b).wait_recv()
            on_left(b).wait_recv()

    count = len(ORDER)
    for step in range(count + 2):
        if step < count:
            arrive(*ORDER[step])
            multiply(*ORDER[step])
        if 1 <= step < count + 1:
            add_x(*ORDER[step - 1])
        if step >= 2:
            add_z(*ORDER[step - 2])

    sums = []
    for b in range(2):
        for other in range(2):
            for q in range(2):
                pltpu.make_async_copy(
                    f_in.at[b, other, q], f_in.at[b, other, q], f_recv.at[b, other, q]
                ).wait()
        sums.append((f_in[b, 0] + f_in[b, 1]).reshape(ROWS, HEAD))
    summed, replay = sums

    mask = kept(0)
    lanes = mask[:, 0:128]
    for j in range(1, 6):
        lanes = lanes + mask[:, j * 128 : (j + 1) * 128]
    scal[0, 0] = jnp.concatenate(
        [
            jnp.sum(summed * replay, axis=0, keepdims=True),
            jnp.sum(replay * replay, axis=0, keepdims=True),
            lanes,
            jnp.zeros((5, 128), jnp.float32),
        ],
        axis=0,
    )

    def s_copy(k, d):
        return remote(
            scal.at[k, 0],
            scal.at[k, d],
            s_send.at[k, d],
            s_recv.at[k, d],
            (z_peer, xc_peer, y_peer)[k](d),
        )

    for k in range(3):
        for d in range(7, 0, -1):
            s_copy(k, d).start()
        for d in range(1, 8):
            s_copy(k, d).wait_recv()
        total = scal[k, 0]
        for d in range(1, 8):
            total = total + scal[k, d]
        scal[k + 1, 0] = total
    totals = jnp.sum(total, axis=1, keepdims=True)
    valid_count = totals[2:3] * 0.125
    inner_sum = totals[0:1] / valid_count
    energy = totals[1:2]
    factor = jnp.minimum(inner_sum, 0.0) / (energy + norm_eps)

    for copy in state_loads:
        copy.wait()
    projected = summed / valid_count - factor * replay
    moment = beta_first * state[1] + (1.0 - beta_first) * projected
    spread = beta_second * state[2] + (1.0 - beta_second) * projected * projected
    fix_first = 1.0 - beta_first**step_number
    fix_second = 1.0 - beta_second**step_number
    update = moment / fix_first / (jnp.sqrt(spread / fix_second) + adam_eps)
    weight = state[0] - learn_rate * (update + decay_rate * state[0])
    gathered[z, yl, x] = weight.astype(jnp.bfloat16)

    def gz_copy(d):
        return remote(
            gathered.at[z, yl, x],
            gathered.at[z, yl, x],
            g_send.at[d],
            g_recv.at[d],
            z_peer(d),
        )

    def gz_in(d):
        block = gathered.at[(z + 8 - d) % 8, yl, x]
        return remote(block, block, g_send.at[d], g_recv.at[d], z_peer(d))

    def gy_copy(src_yl):
        block = gathered.at[:, src_yl, x]
        return remote(block, block, g_send.at[0], g_recv.at[0], device(yl=1 - yl))

    def gx_copy(k, src_yl, src_x, d):
        block = gathered.at[:, src_yl, src_x]
        i = 8 + 4 * k + d
        return remote(block, block, g_send.at[i], g_recv.at[i], x_peer(d))

    for d in (4, 3, 5, 2, 6, 1, 7):
        gz_copy(d).start()
    new_master[...] = weight
    new_first[...] = moment
    new_second[...] = spread
    for d in range(1, 8):
        gz_in(d).wait_recv()
    gy_copy(yl).start()
    for d in (2, 1, 3):
        gx_copy(0, yl, x, d).start()
    gy_copy(1 - yl).wait_recv()
    for d in (2, 1, 3):
        gx_copy(1, 1 - yl, x, d).start()
    for d in range(1, 4):
        gx_copy(0, yl, (x + 4 - d) % 4, d).wait_recv()
        gx_copy(1, 1 - yl, (x + 4 - d) % 4, d).wait_recv()

    for b in range(2):
        pair(b).wait_send()
        for h in range(2):
            to_right(b, h).wait_send()
            to_left(b, h).wait_send()
        on_right(b).wait_send()
        on_left(b).wait_send()
        for rel in range(4):
            for d in range(1, 4):
                x_copy(b, rel, d).wait_send()
            for d in range(1, 8):
                z_copy(b, rel, d).wait_send()
            if rel == OWN:

                @pl.when(jnp.logical_not(goal_self))
                def _():
                    f_copy(b, rel).wait_send()

            else:
                f_copy(b, rel).wait_send()
    for d in range(1, 8):
        for k in range(3):
            s_copy(k, d).wait_send()
        gz_copy(d).wait_send()
    gy_copy(yl).wait_send()
    for d in range(1, 4):
        gx_copy(0, yl, x, d).wait_send()
        gx_copy(1, 1 - yl, x, d).wait_send()


def on_device(
    current_acts,
    current_cot,
    current_ids,
    replay_acts,
    replay_cot,
    replay_ids,
    master_weight,
    first_moment,
    second_moment,
):
    hbm = pl.BlockSpec(memory_space=pl.ANY)
    vmem = pl.BlockSpec(memory_space=pltpu.VMEM)
    rows = jax.ShapeDtypeStruct((ROWS, HEAD), jnp.float32)
    dma = pltpu.SemaphoreType.DMA
    new_master, new_first, new_second, gathered = pl.pallas_call(
        kernel,
        out_shape=(
            rows,
            rows,
            rows,
            jax.ShapeDtypeStruct((8, 2, 4, ROWS, HEAD), jnp.bfloat16),
        ),
        in_specs=[hbm, hbm, vmem, hbm, hbm, vmem, hbm, hbm, hbm],
        out_specs=(vmem, vmem, vmem, vmem),
        scratch_shapes=[
            pltpu.VMEM((2, TOK, FEAT), jnp.bfloat16),
            pltpu.VMEM((2, 2, 4, 2 * ROWS, TOK), jnp.bfloat16),
            pltpu.VMEM((2, 4, TOK, HEAD), jnp.bfloat16),
            pltpu.VMEM((2, 4, 256, HEAD), jnp.float32),
            pltpu.VMEM((2, 4, 4, 256, HEAD), jnp.bfloat16),
            pltpu.VMEM((2, 4, 4, 256, HEAD), jnp.bfloat16),
            pltpu.VMEM((2, 4, 8, 32, HEAD), jnp.float32),
            pltpu.VMEM((2, 4, 8, 32, HEAD), jnp.float32),
            pltpu.VMEM((2, 4, 32, HEAD), jnp.float32),
            pltpu.VMEM((2, 2, 2, 32, HEAD), jnp.float32),
            pltpu.VMEM((3, ROWS, HEAD), jnp.float32),
            pltpu.VMEM((4, 8, 8, HEAD), jnp.float32),
            dma((7,)),
            dma((2,)),
            dma((2,)),
            dma((2, 3, 2)),
            dma((2, 3, 2)),
            dma((2, 4, 4)),
            dma((2, 4, 4)),
            dma((2, 4, 8)),
            dma((2, 4, 8)),
            dma((2, 4)),
            dma((2, 2, 2)),
            dma((3, 8)),
            dma((3, 8)),
            dma((16,)),
            dma((16,)),
        ],
        compiler_params=pltpu.CompilerParams(
            collective_id=0,
            has_side_effects=True,
            vmem_limit_bytes=40 * 1024 * 1024,
        ),
    )(
        current_acts,
        current_cot,
        current_ids.reshape(1, TOK),
        replay_acts,
        replay_cot,
        replay_ids.reshape(1, TOK),
        master_weight,
        first_moment,
        second_moment,
    )
    return (new_master, new_first, new_second, gathered.reshape(64 * ROWS, HEAD))


def solution(mesh):
    placed = (
        P("dp", "tensor"),
        P("dp", "tensor"),
        P("dp"),
        P("dp", "tensor"),
        P("dp", "tensor"),
        P("dp"),
        P("dp", "tensor"),
        P("dp", "tensor"),
        P("dp", "tensor"),
    )
    return jax.shard_map(
        on_device,
        mesh=mesh,
        in_specs=placed,
        out_specs=(P("dp", "tensor"), P("dp", "tensor"), P("dp", "tensor"), P(None, "tensor")),
        check_vma=False,
    )
```

time: 1190 us -> 110 us (0.09)
  the two profiles are of different devices: /device:TPU:16 before, /device:TPU:8 now
where the time goes in v1:
time: 110 us
  Pallas kernels  99.4 us (90%)
  local copies, waits for them, and re-layouts  9.9 us (9%)
    pallas_call x1, Pallas kernels, on_device(): pl.pallas_call(kernel, out_shape=(rows, rows, rows, jax.ShapeDtypeStruct(...  99.4 us
    unnamed x20, local copies, waits for them, and re-layouts  9.21 us

profile of v1, /device:TPU:8, one launch (start us, length us, event | category | flops | bytes accessed | tf_op | source)
XLA Modules:
  0.0 110.0 jit_solution(1162655240329130159)
XLA Ops:
  0.6 0.0 copy-start.7
  0.6 0.7 reshape.17.cur_ids
  1.3 0.0 copy-done.7
  1.3 0.0 copy-start
  1.4 1.1 %copy-done = bf16[768,512]{1,0:T(8,128)(2,1)S(1)} copy-done((bf16[768,512]{1,0:T(8,128)(2,1)S(1)}, bf16[768,512]{1,0:T(8,128)(2,1)}, u32[]{:S(2)}) %copy-start) | copy-done | bytes 786456
  2.5 0.0 copy-start.1
  2.5 1.1 %copy-done.1 = bf16[768,512]{1,0:T(8,128)(2,1)S(1)} copy-done((bf16[768,512]{1,0:T(8,128)(2,1)S(1)}, bf16[768,512]{1,0:T(8,128)(2,1)}, u32[]{:S(2)}) %copy-start.1) | copy-done | bytes 786456
  3.6 0.0 copy-start.2
  3.6 0.9 copy-done.2
  4.5 0.0 copy-start.3
  4.5 0.9 copy-done.3
  5.5 0.0 copy-start.4
  5.5 0.8 copy-done.4
  6.2 0.0 copy-start.5
  6.2 0.8 copy-done.5
  7.0 0.0 copy-start.6
  7.0 0.8 copy-done.6
  7.7 99.4 %shard_map.120 = (f32[64,128]{1,0:T(8,128)S(1)}, f32[64,128]{1,0:T(8,128)S(1)}, f32[64,128]{1,0:T(8,128)S(1)}, bf16[8,2,4,64,128]{4,3,2,1,0:T(8,128)(2,1)S(1)}) custom-call(bf16[768,512]{1,0:T(8,128)(2,1)S(1)} %copy-done, bf16[768,128]{1,0:T(8,128)(2,1)S(1)} %copy-done.2, s32[1,768]{1,0:T(1,128)S(1)} %reshape.17.cur_ids, bf16[768,512]{1,0:T(8,128)(2,1)S(1)} %copy-done.1, ...), custom_call_target="tpu_custom_call" | custom-call | tf_op jit(solution)/shard_map/pallas_call | solution.py:497
  107.2 0.6 copy.17
  107.8 0.6 copy.18
  108.4 0.6 copy.19
  109.0 1.0 copy.20
  (1 shorter events, 0.0 us)
Async XLA Ops:
  0.6 0.7 copy-start.7
  1.3 1.1 %copy-start = (bf16[768,512]{1,0:T(8,128)(2,1)S(1)}, bf16[768,512]{1,0:T(8,128)(2,1)}, u32[]{:S(2)}) copy-start(bf16[768,512]{1,0:T(8,128)(2,1)} %cur_acts.1) | copy-start | bytes 2359300
  2.5 1.1 %copy-start.1 = (bf16[768,512]{1,0:T(8,128)(2,1)S(1)}, bf16[768,512]{1,0:T(8,128)(2,1)}, u32[]{:S(2)}) copy-start(bf16[768,512]{1,0:T(8,128)(2,1)} %rep_acts.1) | copy-start | bytes 2359300
  3.6 0.9 copy-start.2
  4.5 0.9 copy-start.3
  5.5 0.8 copy-start.4
  6.2 0.8 copy-start.5
  7.0 0.8 copy-start.6
